TPU v7x, 32 devices: a whole 2x2x4 slice. The times are simulated.
32 devices in a mesh: groups: 2 (over y), blk: 8 (over z, x), narrow: 2 (over core).
Axes of the slice: x: 2, y: 2, z: 4, core: 2. Of those that a mesh axis runs over, the one named last changes fastest.
Arguments:
- tokens: bfloat16 [256, 8192], P(('groups', 'blk'), 'narrow'), parts along dimension 0, may hold values from -6 to 6
- gate_weight: bfloat16 [8192, 24576], P('narrow', 'blk'), may hold values from -0.09375 to 0.09375
- up_weight: bfloat16 [8192, 24576], P('narrow', 'blk'), may hold values from -0.09375 to 0.09375
- gate_mask: int32 [64, 192], P('narrow', 'blk'), may hold values from 0 to 1, as said below
- up_mask: int32 [64, 192], P('narrow', 'blk'), may hold values from 0 to 1, as said below
- down_weight: bfloat16 [24576, 8192], P('blk', 'narrow'), may hold values from -0.0546875 to 0.0546875
- down_mask: int32 [192, 64], P('blk', 'narrow'), may hold values from 0 to 1, as said below
Outputs:
- mixed: bfloat16 [256, 8192], P(('groups', 'blk'), 'narrow'), parts along dimension 0
There are 2 independent parts, one for each index of `groups`. A program takes and returns all parts, laid end to end along the dimension named above; an argument that names none is the same for every part. Nothing has to cross between parts.
Inputs may be any that keep to these rules, and one draw needn't show every extreme that they name: `gate_mask`: entries are 0 or 1; the share kept may differ from one column of blocks (gate, up) or row of blocks (down) to the next. `up_mask`: as gate_mask. `down_mask`: as gate_mask.
All inputs are finite; a program needn't handle non-finite values.
Results may differ from a plain program's by a relative error of at most 0.0049.
Values may be sent and summed in bfloat16 or wider, within the bound.
A program may use at most 320 MiB of HBM per device.

v0:
```python
import jax
import jax.numpy as jnp
from jax import lax
from jax.sharding import PartitionSpec as P


def expand(weight, mask):
    rows, cols = mask.shape
    side = weight.shape[0] // rows
    tiled = weight.reshape(rows, side, cols, side) * mask[:, None, :, None].astype(weight.dtype)
    return tiled.reshape(weight.shape)


def local(tokens, gate_weight, up_weight, gate_mask, up_mask, down_weight, down_mask):
    width = gate_weight.shape[1]
    both_kept = jnp.concatenate(
        [expand(gate_weight, gate_mask), expand(up_weight, up_mask)], axis=1
    )
    partial_sums = jnp.dot(
        lax.all_gather(tokens, "blk", axis=0, tiled=True),
        both_kept,
        preferred_element_type=jnp.float32,
    )
    totals = lax.psum(partial_sums, "narrow")
    hidden = (jax.nn.silu(totals[:, :width]) * totals[:, width:]).astype(jnp.bfloat16)
    down_kept = expand(down_weight, down_mask)
    mixed = lax.psum_scatter(
        jnp.dot(hidden, down_kept, preferred_element_type=jnp.float32),
        "blk",
        scatter_dimension=0,
        tiled=True,
    )
    return mixed.astype(jnp.bfloat16)


def solution(mesh):
    in_specs = (
        P(("groups", "blk"), "narrow"),
        P("narrow", "blk"),
        P("narrow", "blk"),
        P("narrow", "blk"),
        P("narrow", "blk"),
        P("blk", "narrow"),
        P("blk", "narrow"),
    )
    out_specs = P(("groups", "blk"), "narrow")
    return jax.shard_map(local, mesh=mesh, in_specs=in_specs, out_specs=out_specs, check_vma=False)
```

profile of v0, /device:TPU:0, one launch (start us, length us, event | category | flops | bytes accessed | tf_op | source)
XLA Modules:
  0.0 224.5 jit_solution(572123930493155277)
XLA Ops:
  6.5 0.0 all-gather.2.cloned.1.call-start
  6.5 0.7 all-gather.2.cloned.1.call-update
  7.3 0.0 all-reduce.2.cloned.1.call-start
  7.3 0.7 convert_element_type.18
  8.0 0.1 copy.8
  8.1 0.7 convert_element_type.19
  8.8 0.1 copy.9
  8.9 4.2 %mul.40 = bf16[32,128,24,128]{3,2,1,0:T(8,128)(2,1)S(1)} broadcast(bf16[32,24]{1,0:T(8,128)(2,1)S(1)} %copy.8), dimensions={0,2} | broadcast | bytes 25167360 | tf_op jit(solution)/shard_map/mul | solution.py:10
  13.1 8.7 %mul.43 = bf16[32,128,24,128]{3,2,1,0:T(8,128)(2,1)} broadcast(bf16[32,24]{1,0:T(8,128)(2,1)S(1)} %copy.9), dimensions={0,2} | broadcast | bytes 25167360 | tf_op jit(solution)/shard_map/mul | solution.py:10
  21.9 45.8 %bitcast_multiply_fusion.2 = (bf16[4096,3072]{1,0:T(8,128)(2,1)}, bf16[4096,3072]{1,0:T(8,128)(2,1)}) fusion(bf16[4096,3072]{1,0:T(8,128)(2,1)} %param.9, bf16[512,8,24,128]{3,2,1,0:T(8,128)(2,1)} %bitcast.17, bf16[4096,3072]{1,0:T(8,128)(2,1)} %param.8, bf16[512,8,24,128]{3,2,1,0:T(8,128)(2,1)S(1)} %bitcast.16), kind=kLoop, calls=%fused_computation.7 | loop fusion | flops 25165824 | bytes 150994944 | tf_op jit(solution)/shard_map/mul | solution.py:10
  67.7 0.0 all-gather.2.cloned.1.call-done
  67.7 0.0 copy-start
  67.7 21.7 %fusion.6 = f32[128,6144]{0,1:T(8,128)} fusion(bf16[128,4096]{1,0:T(8,128)(2,1)} %all-gather.2.cloned.1.call-done, bf16[4096,3072]{1,0:T(8,128)(2,1)} %get-tuple-element.5, bf16[4096,3072]{1,0:T(8,128)(2,1)} %get-tuple-element.6), kind=kOutput, calls=%fused_computation.9 | convolution fusion | flops 6543114240 | bytes 54525952 | tf_op jit(solution)/shard_map/dot_general | solution.py:19
  89.4 0.0 all-reduce.2.cloned.1.call-update
  89.4 0.0 reduce-scatter.2.cloned.1.call-start
  89.4 0.0 copy-done
  89.4 26.0 %all-reduce.2.cloned.1.call-done = f32[128,6144]{0,1:T(8,128)} async-done(((f32[128,6144]{0,1:T(8,128)}), f32[128,6144]{0,1:T(8,128)}) %all-reduce.2.cloned.1.call-update) | async-done | bytes 3145744 | tf_op jit(solution)/shard_map/psum | solution.py:24
  115.4 0.0 copy-start.1
  115.4 8.8 %mul.48 = bf16[24,128,32,128]{3,2,1,0:T(8,128)(2,1)} broadcast(bf16[24,32]{1,0:T(8,128)(2,1)S(1)} %convert_element_type.21), dimensions={0,2} | broadcast | bytes 25167360 | tf_op jit(solution)/shard_map/mul | solution.py:10
  124.2 0.0 copy-done.1
  124.2 23.2 %fusion.4 = f32[128,4096]{1,0:T(8,128)} fusion(bf16[3072,4096]{1,0:T(8,128)(2,1)} %param.12, bf16[384,8,32,128]{3,2,1,0:T(8,128)(2,1)} %bitcast.18, f32[128,6144]{0,1:T(8,128)S(1)} %copy-done.1), kind=kOutput, calls=%fused_computation.5 | convolution fusion | flops 3236167680 | bytes 55574528 | tf_op jit(solution)/shard_map/dot_general | solution.py:28
  147.4 0.0 reduce-scatter.2.cloned.1.call-update
  147.4 69.0 %reduce-scatter.2.cloned.1.call-done = f32[16,4096]{1,0:T(8,128)} async-done(((f32[128,4096]{1,0:T(8,128)}), f32[16,4096]{1,0:T(8,128)}) %reduce-scatter.2.cloned.1.call-update) | async-done | bytes 262160 | tf_op jit(solution)/shard_map/reduce_scatter | solution.py:27
  216.4 1.6 convert_element_type.22
  (1 shorter events, 0.0 us)
Async XLA Ops:
  6.5 61.1 %all-gather.2.cloned.1.call-start = ((), (), s32[]{:S(2)}) async-start(), calls=%async_computation.1 | async-start | bytes 1179648 | tf_op jit(solution)/shard_map/all_gather | solution.py:20
  7.3 108.2 %all-reduce.2.cloned.1.call-start = ((), (), s32[]{:S(2)}) async-start(), calls=%async_computation.2 | async-start | bytes 6291456 | tf_op jit(solution)/shard_map/psum | solution.py:24
  67.7 21.8 %copy-start = (s32[24,32]{1,0:T(8,128)S(1)}, s32[24,32]{1,0:T(8,128)}, u32[]{:S(2)}) copy-start(s32[24,32]{1,0:T(8,128)} %param.13) | copy-start | bytes 9220
  89.4 127.0 %reduce-scatter.2.cloned.1.call-start = ((), (), s32[]{:S(2)}) async-start(), calls=%async_computation.3 | async-start | bytes 2359296 | tf_op jit(solution)/shard_map/reduce_scatter | solution.py:27
  115.4 8.8 %copy-start.1 = (f32[128,6144]{0,1:T(8,128)S(1)}, f32[128,6144]{0,1:T(8,128)}, u32[]{:S(2)}) copy-start(f32[128,6144]{0,1:T(8,128)} %all-reduce.2.cloned.1.call-done) | copy-start | bytes 9437188
Sparse Core Ops, SparseCore 0:
  9.5 42.9 all-gather.1
  89.5 25.9 all-reduce.1
  147.5 68.7 reduce-scatter.1
where the time goes:
time: 225 us
  waiting for transfers between devices  95.7 us (43%)
  other arithmetic  48.8 us (22%)
  matrix products  44.9 us (20%)
  local copies, waits for them, and re-layouts  21.9 us (10%)
  between operations  13.1 us (6%)
    reduce_scatter x1, waiting for transfers between devices, local(): lax.psum_scatter(jnp.dot(hidden, down_kept, preferred_element_type=jnp.fl...  69 us
    mul x1, other arithmetic, expand(): weight.reshape(rows, side, cols, side)  45.8 us
    psum x1, waiting for transfers between devices, local(): totals = lax.psum(partial_sums, 'narrow')  26 us
    dot_general x1, matrix products, local(): jnp.dot(hidden, down_kept, preferred_element_type=jnp.float32)  23.2 us
    mul x3, local copies, waits for them, and re-layouts, expand(): weight.reshape(rows, side, cols, side)  21.7 us
    dot_general x1, matrix products, local(): jnp.dot(lax.all_gather(tokens, 'blk', axis=0, tiled=True), both_kept, pre...  21.7 us
  transfers between devices with their start and end apart: 3, of which 2 were waited for; matrix products, arithmetic and copies ran while one was open for 27% of the time, Pallas kernels for 0%

commit v1 on v0

v1 whole, which is shorter than its diff:
```python
import functools

import jax
import jax.numpy as jnp
from jax import lax
from jax.experimental import pallas as pl
from jax.experimental.pallas import tpu as pltpu
from jax.sharding import PartitionSpec as P

MESH = pl.DeviceIdType.MESH
BF = jnp.bfloat16
F32 = jnp.float32


def kernel(
    cfg,
    tok, gw, uw, gm, um, dw, dm, out,
    x, wg, wu, wd, gx, ux, dx, accg, accu, exs, exr, hid, pt, sx, rx, own, sa, ra, own2,
    g_sem, u_sem, d_sem, t_sem,
    a_send, a_recv, f_send, f_recv, e_send, e_recv, x_send, x_recv, z_send, z_recv,
):
    A, B, TR, M, MB, K, F, D, C, KC, S, KS, SD, TC, TN, BS = cfg
    blk, nar = lax.axis_index("blk"), lax.axis_index("narrow")
    a, b = lax.div(blk, B), lax.rem(blk, B)
    GR = A * TR
    NS, NT, T, SPC = K // KS, F // TN, D // TC, KC // KS

    def a_peer(d):
        return lax.rem(a + d, A)

    def b_peer(e):
        return lax.rem(b + e, B)

    def slab(s):
        slot = lax.rem(s, S)
        rows = pl.ds(pl.multiple_of(s * KS, KS), KS)
        return (
            pltpu.make_async_copy(gw.at[rows, :], wg.at[slot], g_sem.at[slot]),
            pltpu.make_async_copy(uw.at[rows, :], wu.at[slot], u_sem.at[slot]),
        )

    def down(c):
        slot = lax.rem(c, SD)
        cols = pl.ds(pl.multiple_of(c * TC, TC), TC)
        return pltpu.make_async_copy(dw.at[:, cols], wd.at[slot], d_sem.at[slot])

    p0 = pl.multiple_of((b * A + a) * TR, TR)
    g0 = pl.multiple_of(b * GR, GR)

    def gather(c, d):
        cols = pl.ds(c * KC, KC)
        return pltpu.make_async_remote_copy(
            src_ref=tok.at[:, cols], dst_ref=x.at[pl.ds(p0, TR), cols],
            send_sem=a_send.at[c, d - 1], recv_sem=a_recv.at[c, d - 1],
            device_id={"blk": a_peer(d) * B + b}, device_id_type=MESH)

    def gather_in(c, d):
        cols = pl.ds(c * KC, KC)
        src = lax.rem(a - d + A, A)
        r = pl.multiple_of((b * A + src) * TR, TR)
        return pltpu.make_async_remote_copy(
            src_ref=tok.at[:, cols], dst_ref=x.at[pl.ds(r, TR), cols],
            send_sem=a_send.at[c, d - 1], recv_sem=a_recv.at[c, d - 1],
            device_id={"blk": a_peer(d) * B + b}, device_id_type=MESH)

    def forward(c, e, r):
        cols = pl.ds(c * KC, KC)
        return pltpu.make_async_remote_copy(
            src_ref=x.at[pl.ds(g0, GR), cols], dst_ref=x.at[pl.ds(r, GR), cols],
            send_sem=f_send.at[c, e - 1], recv_sem=f_recv.at[c, e - 1],
            device_id={"blk": a * B + b_peer(e)}, device_id_type=MESH)

    def forward_in(c, e):
        return forward(c, e, pl.multiple_of(lax.rem(b - e + B, B) * GR, GR))

    def exchange(j):
        return pltpu.make_async_remote_copy(
            src_ref=exs.at[j], dst_ref=exr.at[j],
            send_sem=e_send.at[j], recv_sem=e_recv.at[j],
            device_id={"narrow": 1 - nar}, device_id_type=MESH)

    def to_b(c, e):
        r = pl.multiple_of(b_peer(e) * GR, GR)
        return pltpu.make_async_remote_copy(
            src_ref=sx.at[c, pl.ds(r, GR), :], dst_ref=rx.at[c, e - 1],
            send_sem=x_send.at[c, e - 1], recv_sem=x_recv.at[c, e - 1],
            device_id={"blk": a * B + b_peer(e)}, device_id_type=MESH)

    def to_a(c, d):
        r = pl.multiple_of(a_peer(d) * TR, TR)
        return pltpu.make_async_remote_copy(
            src_ref=sa.at[c, pl.ds(r, TR), :], dst_ref=ra.at[c, d - 1],
            send_sem=z_send.at[c, d - 1], recv_sem=z_recv.at[c, d - 1],
            device_id={"blk": a_peer(d) * B + b}, device_id_type=MESH)

    mine = pltpu.make_async_copy(tok, x.at[pl.ds(p0, TR), :], t_sem)
    mine.start()
    for s in range(min(S, NS)):
        for cp in slab(s):
            cp.start()

    barrier = pltpu.get_barrier_semaphore()
    for d in range(1, A):
        pl.semaphore_signal(barrier, inc=1, device_id={"blk": a_peer(d) * B + b}, device_id_type=MESH)
    for e in range(1, B):
        pl.semaphore_signal(barrier, inc=1, device_id={"blk": a * B + b_peer(e)}, device_id_type=MESH)
    pl.semaphore_signal(barrier, inc=1, device_id={"narrow": 1 - nar}, device_id_type=MESH)
    pl.semaphore_wait(barrier, A + B - 1)

    for c in range(C):
        for d in range(1, A):
            gather(c, d).start()

    for mask, spread in ((gm, gx), (um, ux), (dm, dx)):
        m = mask[...].astype(F32)
        for n in range(m.shape[1]):
            spread[:, n * BS:(n + 1) * BS] = jnp.broadcast_to(m[:, n:n + 1], (m.shape[0], BS))
    accg[...] = jnp.zeros_like(accg)
    accu[...] = jnp.zeros_like(accu)

    def relay(c):
        if c == 0:
            mine.wait()
        for d in range(1, A):
            gather_in(c, d).wait_recv()
        for e in range(1, B):
            forward(c, e, g0).start()

    def masked(w, spread, row, cols):
        rows, width = w.shape
        parts = []
        for i in range(rows // BS):
            m = spread[pl.ds(row + i, 1), cols]
            m = jnp.broadcast_to(m, (16, width)).astype(BF)
            wi = w[i * BS:(i + 1) * BS].reshape(BS // 16, 16, width) * m[None]
            parts.append(wi.reshape(BS, width))
        return jnp.concatenate(parts, axis=0)

    KD = 2 * BS

    def product(left, rows, first, w, slot, cols, mcols, spread, row0, depth):
        kd = KD if depth % KD == 0 else BS
        total = None
        for k in range(depth // kd):
            lhs = left[rows, pl.ds(first + k * kd, kd)]
            rhs = masked(w[slot, k * kd:(k + 1) * kd, cols], spread, row0 + k * (kd // BS), mcols)
            part = jnp.dot(lhs, rhs, preferred_element_type=F32)
            total = part if total is None else total + part
        return total

    def slab_step(s, last):
        for cp in slab(s):
            cp.wait()
        slot = lax.rem(s, S)
        first = pl.multiple_of(s * KS, KS)

        def tile(j, _):
            cols = pl.ds(pl.multiple_of(j * TN, TN), TN)
            for i in range(M // MB):
                rows = pl.ds(i * MB, MB)
                for q, (w, spread, acc) in enumerate(((wg, gx, accg), (wu, ux, accu))):
                    t = product(x, rows, first, w, slot, cols, cols, spread, s * (KS // BS), KS)
                    t = t + acc[rows, cols]
                    acc[rows, cols] = t
                    if last:
                        exs[j, q, rows, :] = t.astype(BF)
            if last:
                exchange(j).start()
            return 0

        lax.fori_loop(0, NT, tile, 0)

    relay(0)
    for c in range(C):
        if c + 1 < C:
            relay(c + 1)
        for e in range(1, B):
            forward_in(c, e).wait_recv()
        for i in range(SPC):
            s = c * SPC + i
            slab_step(s, s == NS - 1)
            if s + S < NS:
                for cp in slab(s + S):
                    cp.start()
            else:
                n = s + S - NS
                lo, hi = n * SD // min(S, NS), (n + 1) * SD // min(S, NS)
                for t in range(lo, min(hi, T)):
                    down(t).start()

    def finish(j, _):
        exchange(j).wait_recv()
        cols = pl.ds(pl.multiple_of(j * TN, TN), TN)
        for i in range(M // MB):
            rows = pl.ds(i * MB, MB)
            g = accg[rows, cols] + exr[j, 0, rows, :].astype(F32)
            u = accu[rows, cols] + exr[j, 1, rows, :].astype(F32)
            hid[rows, cols] = (g / (1.0 + jnp.exp(-g)) * u).astype(BF)
        return 0

    lax.fori_loop(0, NT, finish, 0)

    def step(c, _):
        @pl.when(c < T)
        def _():
            down(c).wait()
            slot = lax.rem(c, SD)
            for i in range(M // MB):
                rows = pl.ds(i * MB, MB)

                def part(h, _):
                    cols = pl.ds(pl.multiple_of(h * TN, TN), TN)
                    mcols = pl.ds(pl.multiple_of(c * TC + h * TN, TN), TN)
                    t = product(hid, rows, 0, wd, slot, cols, mcols, dx, 0, F)
                    pt[rows, cols] = t
                    sx[c, rows, cols] = t.astype(BF)
                    return 0

                lax.fori_loop(0, TC // TN, part, 0)
            for e in range(1, B):
                to_b(c, e).start()
            own[c] = pt[pl.ds(g0, GR), :]

            @pl.when(c + SD < T)
            def _():
                down(c + SD).start()

        @pl.when(jnp.logical_and(c >= 1, c <= T))
        def _():
            q = c - 1
            for e in range(1, B):
                to_b(q, e).wait_recv()
            t = own[q]
            for e in range(1, B):
                t = t + rx[q, e - 1].astype(F32)
            own[q] = t
            sa[q] = t.astype(BF)
            for d in range(1, A):
                to_a(q, d).start()
            own2[q] = own[q, pl.ds(pl.multiple_of(a * TR, TR), TR), :]

        @pl.when(c >= 2)
        def _():
            q = c - 2
            for d in range(1, A):
                to_a(q, d).wait_recv()
            t = own2[q]
            for d in range(1, A):
                t = t + ra[q, d - 1].astype(F32)
            out[:, pl.ds(pl.multiple_of(q * TC, TC), TC)] = t.astype(BF)

        return 0

    lax.fori_loop(0, T + 2, step, 0)

    for c in range(C):
        for d in range(1, A):
            gather(c, d).wait_send()
        for e in range(1, B):
            forward(c, e, g0).wait_send()

    def sent(j, _):
        exchange(j).wait_send()
        return 0

    lax.fori_loop(0, NT, sent, 0)

    def sent2(c, _):
        for e in range(1, B):
            to_b(c, e).wait_send()
        for d in range(1, A):
            to_a(c, d).wait_send()
        return 0

    lax.fori_loop(0, T, sent2, 0)


def local(nb, tokens, gate_weight, up_weight, gate_mask, up_mask, down_weight, down_mask):
    TR, K = tokens.shape
    F, D = down_weight.shape
    BS = K // gate_mask.shape[0]
    A = 4 if nb % 4 == 0 else 1
    B = nb // A
    M = TR * nb
    MB = min(M, 128)
    C = 4
    KC = K // C
    KS = KC // 2
    S = 5
    SD = 4
    TC = min(D, 512)
    TN = 256 if F % 256 == 0 else BS
    NT, T = F // TN, D // TC
    GR = A * TR
    cfg = (A, B, TR, M, MB, K, F, D, C, KC, S, KS, SD, TC, TN, BS)
    dma = pltpu.SemaphoreType.DMA
    hbm = pl.BlockSpec(memory_space=pl.ANY)
    vmem = pl.BlockSpec(memory_space=pltpu.VMEM)
    return pl.pallas_call(
        functools.partial(kernel, cfg),
        out_shape=jax.ShapeDtypeStruct((TR, D), BF),
        in_specs=[hbm, hbm, hbm, vmem, vmem, hbm, vmem],
        out_specs=vmem,
        scratch_shapes=[
            pltpu.VMEM((M, K), BF),
            pltpu.VMEM((S, KS, F), BF),
            pltpu.VMEM((S, KS, F), BF),
            pltpu.VMEM((SD, F, TC), BF),
            pltpu.VMEM((K // BS, F), F32),
            pltpu.VMEM((K // BS, F), F32),
            pltpu.VMEM((F // BS, D), F32),
            pltpu.VMEM((M, F), F32),
            pltpu.VMEM((M, F), F32),
            pltpu.VMEM((NT, 2, M, TN), BF),
            pltpu.VMEM((NT, 2, M, TN), BF),
            pltpu.VMEM((M, F), BF),
            pltpu.VMEM((M, TC), F32),
            pltpu.VMEM((T, M, TC), BF),
            pltpu.VMEM((T, max(B - 1, 1), GR, TC), BF),
            pltpu.VMEM((T, GR, TC), F32),
            pltpu.VMEM((T, GR, TC), BF),
            pltpu.VMEM((T, max(A - 1, 1), TR, TC), BF),
            pltpu.VMEM((T, TR, TC), F32),
            dma((S,)), dma((S,)), dma((SD,)), dma(()),
            dma((C, max(A - 1, 1))), dma((C, max(A - 1, 1))),
            dma((C, max(B - 1, 1))), dma((C, max(B - 1, 1))),
            dma((NT,)), dma((NT,)),
            dma((T, max(B - 1, 1))), dma((T, max(B - 1, 1))),
            dma((T, max(A - 1, 1))), dma((T, max(A - 1, 1))),
        ],
        compiler_params=pltpu.CompilerParams(
            collective_id=0, has_side_effects=True, vmem_limit_bytes=62 * 2**20
        ),
        cost_estimate=pl.CostEstimate(
            flops=6 * M * K * F, bytes_accessed=6 * K * F, transcendentals=M * F
        ),
    )(tokens, gate_weight, up_weight, gate_mask, up_mask, down_weight, down_mask)


def solution(mesh):
    in_specs = (
        P(("groups", "blk"), "narrow"),
        P("narrow", "blk"),
        P("narrow", "blk"),
        P("narrow", "blk"),
        P("narrow", "blk"),
        P("blk", "narrow"),
        P("blk", "narrow"),
    )
    out_specs = P(("groups", "blk"), "narrow")
    return jax.shard_map(
        functools.partial(local, mesh.shape["blk"]),
        mesh=mesh, in_specs=in_specs, out_specs=out_specs, check_vma=False,
    )
```

time: 225 us -> 76.7 us (0.34)
  waiting for transfers between devices: 95.7 us -> 0 us
  Pallas kernels: 0 us -> 71.9 us
  other arithmetic: 48.8 us -> 0 us
  matrix products: 44.9 us -> 0 us
  local copies, waits for them, and re-layouts: 21.9 us -> 4.33 us
  between operations: 13.1 us -> 0.01 us
    pallas_call x0 -> x1, Pallas kernels: none -> 71.9 us  [local(): pl.pallas_call(functools.partial(kernel, cfg), out_shape=jax.ShapeDtypeSt...]
    reduce_scatter x1 -> x0, waiting for transfers between devices: 69 us -> none  [local(): lax.psum_scatter(jnp.dot(hidden, down_kept, preferred_element_type=jnp.fl...]
    mul x1 -> x0, other arithmetic: 45.8 us -> none  [expand(): weight.reshape(rows, side, cols, side)]
    dot_general x2 -> x0, matrix products: 44.9 us -> none  [the longest x1 23.2 us: local(): jnp.dot(hidden, down_kept, preferred_element_type=jnp.float32)]
    psum x1 -> x0, waiting for transfers between devices: 26 us -> none  [local(): totals = lax.psum(partial_sums, 'narrow')]
    mul x3 -> x0, local copies, waits for them, and re-layouts: 21.7 us -> none  [expand(): weight.reshape(rows, side, cols, side)]
    unnamed x4 -> x3, local copies, waits for them, and re-layouts: 0.01 us -> 4.33 us
    convert_element_type x4 -> x0, other arithmetic: 3.05 us -> none  [the longest x1 1.62 us: local(): return mixed.astype(jnp.bfloat16)]
  transfers between devices with their start and end apart: 3 -> 0, of which waited for: 2 -> 0; matrix products, arithmetic and copies ran while one was open for 27% -> 0% of each run, Pallas kernels for 0% -> 0%
where the time goes in v1:
time: 76.7 us; the launch traced here: 76.2 us
  Pallas kernels  71.9 us (94%)
  local copies, waits for them, and re-layouts  4.33 us (6%)
    pallas_call x1, Pallas kernels, local(): pl.pallas_call(functools.partial(kernel, cfg), out_shape=jax.ShapeDtypeSt...  71.9 us
    unnamed x3, local copies, waits for them, and re-layouts  4.33 us

profile of v1, /device:TPU:0, one launch (start us, length us, event | category | flops | bytes accessed | tf_op | source)
XLA Modules:
  0.0 76.2 jit_solution(10453466204946648957)
XLA Ops:
  0.0 1.4 %copy.8.gm = s32[32,24]{1,0:T(8,128)} copy(s32[32,24]{0,1:T(8,128)} %param.10) | data formatting | bytes 6144 | tf_op args[3]
  1.4 1.4 %copy.9.um = s32[32,24]{1,0:T(8,128)} copy(s32[32,24]{0,1:T(8,128)} %param.11) | data formatting | bytes 6144 | tf_op args[4]
  2.8 71.9 %shard_map.73 = bf16[16,4096]{1,0:T(8,128)(2,1)} custom-call(bf16[16,4096]{1,0:T(8,128)(2,1)} %tok.1, bf16[4096,3072]{1,0:T(8,128)(2,1)} %gw.1, bf16[4096,3072]{1,0:T(8,128)(2,1)} %uw.1, s32[32,24]{1,0:T(8,128)} %copy.8.gm, s32[32,24]{1,0:T(8,128)} %copy.9.um, bf16[3072,4096]{1,0:T(8,128)(2,1)} %dw.1, s32[24,32]{1,0:T(8,128)} %dm.1), custom_call_target="tpu_custom_call" | custom-call | flops 9663676416 | bytes 75497472 | tf_op jit(solution)/shard_map/pallas_call | solution.py:299
  74.7 1.6 %copy.11 = bf16[16,4096]{1,0:T(8,128)(2,1)} copy(bf16[16,4096]{1,0:T(8,128)(2,1)} %shard_map.73) | data formatting | bytes 262144

commit v2 on v1

--- a/solution.py
+++ b/solution.py
@@ -63,15 +63,22 @@
             send_sem=a_send.at[c, d - 1], recv_sem=a_recv.at[c, d - 1],
             device_id={"blk": a_peer(d) * B + b}, device_id_type=MESH)
 
-    def forward(c, e, r):
+    def forward(c, e, d):
         cols = pl.ds(c * KC, KC)
-        return pltpu.make_async_remote_copy(
-            src_ref=x.at[pl.ds(g0, GR), cols], dst_ref=x.at[pl.ds(r, GR), cols],
-            send_sem=f_send.at[c, e - 1], recv_sem=f_recv.at[c, e - 1],
+        r = pl.multiple_of((b * A + lax.rem(a - d + A, A)) * TR, TR)
+        dst = x.at[pl.ds(r, TR), cols]
+        return pltpu.make_async_remote_copy(
+            src_ref=tok.at[:, cols] if d == 0 else dst, dst_ref=dst,
+            send_sem=f_send.at[c, e - 1, d], recv_sem=f_recv.at[c, e - 1, d],
             device_id={"blk": a * B + b_peer(e)}, device_id_type=MESH)
 
-    def forward_in(c, e):
-        return forward(c, e, pl.multiple_of(lax.rem(b - e + B, B) * GR, GR))
+    def forward_in(c, e, d):
+        cols = pl.ds(c * KC, KC)
+        r = pl.multiple_of((lax.rem(b - e + B, B) * A + lax.rem(a - d + A, A)) * TR, TR)
+        return pltpu.make_async_remote_copy(
+            src_ref=tok.at[:, cols], dst_ref=x.at[pl.ds(r, TR), cols],
+            send_sem=f_send.at[c, e - 1, d], recv_sem=f_recv.at[c, e - 1, d],
+            device_id={"blk": a * B + b_peer(e)}, device_id_type=MESH)
 
     def exchange(j):
         return pltpu.make_async_remote_copy(
@@ -98,6 +105,8 @@
     for s in range(min(S, NS)):
         for cp in slab(s):
             cp.start()
+    for t in range(min(SD, T)):
+        down(t).start()
 
     barrier = pltpu.get_barrier_semaphore()
     for d in range(1, A):
@@ -110,9 +119,12 @@
     for c in range(C):
         for d in range(1, A):
             gather(c, d).start()
+        for e in range(1, B):
+            forward(c, e, 0).start()
 
     for mask, spread in ((gm, gx), (um, ux), (dm, dx)):
         m = mask[...].astype(F32)
+        m = m if spread is dx else m.T
         for n in range(m.shape[1]):
             spread[:, n * BS:(n + 1) * BS] = jnp.broadcast_to(m[:, n:n + 1], (m.shape[0], BS))
     accg[...] = jnp.zeros_like(accg)
@@ -123,8 +135,8 @@
             mine.wait()
         for d in range(1, A):
             gather_in(c, d).wait_recv()
-        for e in range(1, B):
-            forward(c, e, g0).start()
+            for e in range(1, B):
+                forward(c, e, d).start()
 
     def masked(w, spread, row, cols):
         rows, width = w.shape
@@ -136,7 +148,8 @@
             parts.append(wi.reshape(BS, width))
         return jnp.concatenate(parts, axis=0)
 
-    KD = 2 * BS
+    KD = 4 * BS
+    LX, LZ = 2, 5
 
     def product(left, rows, first, w, slot, cols, mcols, spread, row0, depth):
         kd = KD if depth % KD == 0 else BS
@@ -168,25 +181,22 @@
                 exchange(j).start()
             return 0
 
-        lax.fori_loop(0, NT, tile, 0)
+        lax.fori_loop(0, NT, tile, 0, unroll=True)
 
     relay(0)
+    relay(1)
     for c in range(C):
-        if c + 1 < C:
-            relay(c + 1)
+        if c + 2 < C:
+            relay(c + 2)
         for e in range(1, B):
-            forward_in(c, e).wait_recv()
+            for d in range(A):
+                forward_in(c, e, d).wait_recv()
         for i in range(SPC):
             s = c * SPC + i
             slab_step(s, s == NS - 1)
             if s + S < NS:
                 for cp in slab(s + S):
                     cp.start()
-            else:
-                n = s + S - NS
-                lo, hi = n * SD // min(S, NS), (n + 1) * SD // min(S, NS)
-                for t in range(lo, min(hi, T)):
-                    down(t).start()
 
     def finish(j, _):
         exchange(j).wait_recv()
@@ -198,7 +208,7 @@
             hid[rows, cols] = (g / (1.0 + jnp.exp(-g)) * u).astype(BF)
         return 0
 
-    lax.fori_loop(0, NT, finish, 0)
+    lax.fori_loop(0, NT, finish, 0, unroll=True)
 
     def step(c, _):
         @pl.when(c < T)
@@ -225,9 +235,9 @@
             def _():
                 down(c + SD).start()
 
-        @pl.when(jnp.logical_and(c >= 1, c <= T))
+        @pl.when(jnp.logical_and(c >= LX, c < T + LX))
         def _():
-            q = c - 1
+            q = c - LX
             for e in range(1, B):
                 to_b(q, e).wait_recv()
             t = own[q]
@@ -239,9 +249,9 @@
                 to_a(q, d).start()
             own2[q] = own[q, pl.ds(pl.multiple_of(a * TR, TR), TR), :]
 
-        @pl.when(c >= 2)
+        @pl.when(c >= LZ)
         def _():
-            q = c - 2
+            q = c - LZ
             for d in range(1, A):
                 to_a(q, d).wait_recv()
             t = own2[q]
@@ -251,13 +261,14 @@
 
         return 0
 
-    lax.fori_loop(0, T + 2, step, 0)
+    lax.fori_loop(0, T + LZ, step, 0)
 
     for c in range(C):
         for d in range(1, A):
             gather(c, d).wait_send()
         for e in range(1, B):
-            forward(c, e, g0).wait_send()
+            for d in range(A):
+                forward(c, e, d).wait_send()
 
     def sent(j, _):
         exchange(j).wait_send()
@@ -283,13 +294,13 @@
     B = nb // A
     M = TR * nb
     MB = min(M, 128)
-    C = 4
+    C = 8
     KC = K // C
-    KS = KC // 2
+    KS = KC
     S = 5
     SD = 4
     TC = min(D, 512)
-    TN = 256 if F % 256 == 0 else BS
+    TN = 512 if F % 512 == 0 else BS
     NT, T = F // TN, D // TC
     GR = A * TR
     cfg = (A, B, TR, M, MB, K, F, D, C, KC, S, KS, SD, TC, TN, BS)
@@ -323,7 +334,7 @@
             pltpu.VMEM((T, TR, TC), F32),
             dma((S,)), dma((S,)), dma((SD,)), dma(()),
             dma((C, max(A - 1, 1))), dma((C, max(A - 1, 1))),
-            dma((C, max(B - 1, 1))), dma((C, max(B - 1, 1))),
+            dma((C, max(B - 1, 1), A)), dma((C, max(B - 1, 1), A)),
             dma((NT,)), dma((NT,)),
             dma((T, max(B - 1, 1))), dma((T, max(B - 1, 1))),
             dma((T, max(A - 1, 1))), dma((T, max(A - 1, 1))),
@@ -334,7 +345,7 @@
         cost_estimate=pl.CostEstimate(
             flops=6 * M * K * F, bytes_accessed=6 * K * F, transcendentals=M * F
         ),
-    )(tokens, gate_weight, up_weight, gate_mask, up_mask, down_weight, down_mask)
+    )(tokens, gate_weight, up_weight, gate_mask.T, up_mask.T, down_weight, down_mask)
 
 
 def solution(mesh):

time: 76.7 us -> 54 us (0.70)
  Pallas kernels: 71.9 us -> 52.2 us
  local copies, waits for them, and re-layouts: 4.33 us -> 1.57 us
    pallas_call x1, Pallas kernels: 71.9 us -> 52.2 us  [local(): pl.pallas_call(functools.partial(kernel, cfg), out_shape=jax.ShapeDtypeSt...]
    unnamed x3 -> x1, local copies, waits for them, and re-layouts: 4.33 us -> 1.57 us
where the time goes in v2:
time: 54 us; the launch traced here: 53.8 us
  Pallas kernels  52.2 us (97%)
  local copies, waits for them, and re-layouts  1.57 us (3%)
    pallas_call x1, Pallas kernels, local(): pl.pallas_call(functools.partial(kernel, cfg), out_shape=jax.ShapeDtypeSt...  52.2 us
    unnamed x1, local copies, waits for them, and re-layouts  1.57 us

profile of v2, /device:TPU:0, one launch (start us, length us, event | category | flops | bytes accessed | tf_op | source)
XLA Modules:
  0.0 53.8 jit_solution(1075424460861296554)
XLA Ops:
  0.0 52.2 %shard_map.73 = bf16[16,4096]{1,0:T(8,128)(2,1)} custom-call(bf16[16,4096]{1,0:T(8,128)(2,1)} %tok.1, bf16[4096,3072]{1,0:T(8,128)(2,1)} %gw.1, bf16[4096,3072]{1,0:T(8,128)(2,1)} %uw.1, s32[24,32]{1,0:T(8,128)} %bitcast.2, s32[24,32]{1,0:T(8,128)} %bitcast.3, bf16[3072,4096]{1,0:T(8,128)(2,1)} %dw.1, s32[24,32]{1,0:T(8,128)} %dm.1), custom_call_target="tpu_custom_call" | custom-call | flops 9663676416 | bytes 75497472 | tf_op jit(solution)/shard_map/pallas_call | solution.py:310
  52.2 1.6 %copy.9 = bf16[16,4096]{1,0:T(8,128)(2,1)} copy(bf16[16,4096]{1,0:T(8,128)(2,1)} %shard_map.73) | data formatting | bytes 262144
